TPU v7x, 32 devices: a whole 2x2x4 slice. The times are simulated.
32 devices in a mesh: pert: 4 (over z), gene: 8 (over y, x, core).
Axes of the slice: x: 2, y: 2, z: 4, core: 2. Of those that a mesh axis runs over, the one named last changes fastest.
Arguments:
- tensor: bfloat16 [4096, 8, 4096], P('pert', None, 'gene'), may hold values from -2400 to 2400
- pert_factor: bfloat16 [4096, 128], P('pert'), may hold values from -10 to 10
- context_factor: bfloat16 [8, 128], replicated, may hold values from -3 to 3
Outputs:
- gene_factor: bfloat16 [4096, 128], P('gene')
- pert_updated: bfloat16 [4096, 128], P('pert')
All inputs are finite; a program needn't handle non-finite values.
Results may differ from a plain program's by a relative error of at most 0.0042.
Values may be sent and summed in bfloat16 or wider, within the bound.
A program may use at most 64 MiB of HBM per device.

v0:
```python
import jax
import jax.numpy as jnp
from jax import lax
from jax.sharding import PartitionSpec as P

epsilon = 1e-06


def solve_gram(rhs, gram):
    lower = jnp.linalg.cholesky(gram)
    half = lax.linalg.triangular_solve(lower, rhs, left_side=False, lower=True, transpose_a=True)
    return lax.linalg.triangular_solve(lower, half, left_side=False, lower=True, transpose_a=False)


def raw_gram(solved):
    return jnp.dot(
        solved.T, solved, precision=lax.Precision.HIGHEST, preferred_element_type=jnp.float32
    )


def shards(tensor, pert_factor, context_factor):
    rows_i = tensor.shape[0]
    rows_j = tensor.shape[2]
    n_pert = lax.axis_size("pert")
    n_gene = lax.axis_size("gene")
    context32 = context_factor.astype(jnp.float32)
    gram_b = jnp.dot(context_factor.T, context_factor, preferred_element_type=jnp.float32)
    local_gram = jnp.dot(pert_factor.T, pert_factor, preferred_element_type=jnp.float32)
    gene_count = rows_j * n_gene
    tensor_block = tensor
    partial_sum = jnp.einsum(
        "ikj,ir->kjr", tensor_block, pert_factor, preferred_element_type=jnp.float32
    )
    gram_a, mttkrp_c = lax.psum(
        (local_gram, jnp.sum(partial_sum * context32[:, None, :], axis=0)), "pert"
    )
    solved_c = solve_gram(mttkrp_c, gram_a * gram_b)
    gram_s = lax.psum(raw_gram(solved_c), "gene")
    scale_c = jnp.sqrt(jnp.diagonal(gram_s) / gene_count + epsilon)
    gene_factor = (solved_c / scale_c[None, :]).astype(jnp.bfloat16)
    gram_c = gram_s / (scale_c[:, None] * scale_c[None, :])
    gram_pert_mode = gram_c * gram_b
    pert_count = rows_i * n_pert
    tensor_block = tensor
    partial_sum = jnp.einsum(
        "ikj,jr->ikr", tensor_block, gene_factor, preferred_element_type=jnp.float32
    )
    mttkrp_a = lax.psum(jnp.sum(partial_sum * context32[None, :, :], axis=1), "gene")
    solved_a = solve_gram(mttkrp_a, gram_pert_mode)
    squares_a = lax.psum(jnp.sum(solved_a * solved_a, axis=0), "pert")
    scale_a = jnp.sqrt(squares_a / pert_count + epsilon)
    pert_updated = (solved_a / scale_a[None, :]).astype(jnp.bfloat16)
    return (gene_factor, pert_updated)


def solution(mesh):
    return jax.shard_map(
        shards,
        mesh=mesh,
        in_specs=(P("pert", None, "gene"), P("pert", None), P()),
        out_specs=(P("gene", None), P("pert", None)),
        check_vma=False,
    )
```

profile of v0, /device:TPU:0, one launch (start us, length us, event | category | flops | bytes accessed | tf_op | source)
XLA Modules:
  0.0 241.3 jit_solution(14687042638247086162)
XLA Ops:
  7.2 0.0 copy-start
  7.2 0.0 copy-start.2
  7.2 0.0 all-reduce.9.cloned.1.call-start
  7.2 0.7 convert_element_type.9
  8.0 0.2 copy-done
  8.1 0.9 fusion.24
  9.0 13.0 %multiply_reduce_fusion = f32[512,128]{1,0:T(8,128)} fusion(bf16[1024,8,512]{2,1,0:T(8,128)(2,1)} %param.4, f32[8,128]{1,0:T(8,128)S(1)} %convert_element_type.9, bf16[1024,128]{1,0:T(8,128)(2,1)S(1)} %copy-done), kind=kOutput, calls=%fused_computation.7 | convolution fusion | flops 1074724864 | bytes 8916992 | tf_op jit(solution)/shard_map/ikj,ir->kjr/dot_general | solution.py:31
  22.0 0.0 all-reduce.9.cloned.1.call-update
  22.0 0.2 all-reduce.5.cloned.1.call-start
  22.2 39.0 %all-reduce.9.cloned.1.call-done = (f32[512,128]{1,0:T(8,128)}, f32[128,128]{0,1:T(8,128)}) async-done(((f32[512,128]{1,0:T(8,128)}, f32[128,128]{0,1:T(8,128)}), (f32[512,128]{1,0:T(8,128)}, f32[128,128]{0,1:T(8,128)})) %all-reduce.9.cloned.1.call-update) | async-done | bytes 327696 | tf_op jit(solution)/shard_map/psum | solution.py:34
  61.2 0.0 copy-done.2
  61.2 1.1 fusion.23
  62.3 0.1 copy.22
  62.4 11.7 %cholesky.44 = f32[128,128]{1,0:T(8,128)S(1)} custom-call(f32[128,128]{1,0:T(8,128)S(1)} %fusion.22), custom_call_target="Cholesky" | custom-call | tf_op jit(solution)/shard_map/jit(cholesky)/cholesky | solution.py:10
  74.1 0.6 compare_reduce_fusion.1
  74.8 0.7 fusion.11
  75.4 9.8 %custom-call.12 = f32[1,128,128]{1,2,0:T(8,128)S(1)} custom-call(f32[1,128,128]{2,1,0:T(8,128)S(1)} %fusion.11), custom_call_target="InvertDiagBlocksLowerTriangular" | custom-call | tf_op jit(solution)/shard_map/triangular_solve | solution.py:11
  85.2 1.3 fusion.20
  86.6 0.4 fusion.18
  86.9 1.2 fusion.25
  88.2 0.0 all-reduce.5.cloned.1.call-update
  88.2 0.3 all-reduce.7.cloned.1.call-start
  88.5 52.1 %all-reduce.5.cloned.1.call-done = f32[128,128]{0,1:T(8,128)} async-done(((f32[128,128]{0,1:T(8,128)}), f32[128,128]{0,1:T(8,128)}) %all-reduce.5.cloned.1.call-update) | async-done | bytes 65552 | tf_op jit(solution)/shard_map/psum | solution.py:38
  140.6 1.9 gather_fusion
  142.6 0.0 copy-start.1
  142.6 1.0 divide_multiply_fusion
  143.6 0.1 copy.28
  143.7 11.7 %cholesky.55 = f32[128,128]{1,0:T(8,128)S(1)} custom-call(f32[128,128]{1,0:T(8,128)S(1)} %fusion.17), custom_call_target="Cholesky" | custom-call | tf_op jit(solution)/shard_map/jit(cholesky)/cholesky | solution.py:10
  155.4 9.4 %fusion.4 = f32[1024,128]{0,1:T(8,128)S(1)} fusion(bf16[1024,8,512]{2,1,0:T(8,128)(2,1)} %param.4, f32[8,128]{1,0:T(8,128)S(1)} %convert_element_type.9, bf16[512,128]{1,0:T(8,128)(2,1)S(1)} %divide_convert_fusion.1), kind=kOutput, calls=%fused_computation.6 | convolution fusion | flops 1075707904 | bytes 9048064 | tf_op jit(solution)/shard_map/ikj,jr->ikr/dot_general | solution.py:45
  164.9 1.0 copy.34
  165.9 0.0 all-reduce.7.cloned.1.call-update
  165.9 0.6 compare_reduce_fusion
  166.6 0.7 fusion.12
  167.2 9.8 %custom-call.13 = f32[1,128,128]{1,2,0:T(8,128)S(1)} custom-call(f32[1,128,128]{2,1,0:T(8,128)S(1)} %fusion.12), custom_call_target="InvertDiagBlocksLowerTriangular" | custom-call | tf_op jit(solution)/shard_map/triangular_solve | solution.py:11
  177.0 43.1 %all-reduce.7.cloned.1.call-done = f32[1024,128]{1,0:T(8,128)} async-done(((f32[1024,128]{1,0:T(8,128)}), f32[1024,128]{1,0:T(8,128)}) %all-reduce.7.cloned.1.call-update) | async-done | bytes 524304 | tf_op jit(solution)/shard_map/psum | solution.py:48
  220.2 1.6 fusion.15
  221.8 0.6 multiply_reduce_fusion.1
  222.4 0.0 copy-done.1
  222.4 11.6 %psum.39 = f32[128]{0:T(128)S(1)} all-reduce(f32[128]{0:T(128)S(1)} %get-tuple-element.7), channel_id=1, replica_groups=mesh['pert'=4,'gene'=8] {'pert'}, use_global_device_ids=true, to_apply=%region_9.11 | all-reduce | flops 128 | bytes 1024 | tf_op jit(solution)/shard_map/psum | solution.py:50
  234.0 0.8 divide_convert_fusion
  (8 shorter events, 0.2 us)
Async XLA Ops:
  7.2 1.0 copy-start
  7.2 54.0 %copy-start.2 = (bf16[8,128]{1,0:T(8,128)(2,1)S(1)}, bf16[8,128]{1,0:T(8,128)(2,1)}, u32[]{:S(2)}) copy-start(bf16[8,128]{1,0:T(8,128)(2,1)} %param.6) | copy-start | bytes 6148
  7.2 54.0 %all-reduce.9.cloned.1.call-start = ((), (), s32[]{:S(2)}) async-start(), calls=%async_computation.2 | async-start | bytes 655360 | tf_op jit(solution)/shard_map/psum | solution.py:34
  22.0 118.6 %all-reduce.5.cloned.1.call-start = ((), (), s32[]{:S(2)}) async-start(), calls=%async_computation | async-start | bytes 131072 | tf_op jit(solution)/shard_map/psum | solution.py:38
  88.2 132.0 %all-reduce.7.cloned.1.call-start = ((), (), s32[]{:S(2)}) async-start(), calls=%async_computation.1 | async-start | bytes 1048576 | tf_op jit(solution)/shard_map/psum | solution.py:48
  142.6 79.8 %copy-start.1 = (bf16[512,128]{1,0:T(8,128)(2,1)}, bf16[512,128]{1,0:T(8,128)(2,1)S(1)}, u32[]{:S(2)}) copy-start(bf16[512,128]{1,0:T(8,128)(2,1)S(1)} %divide_convert_fusion.1) | copy-start | bytes 393220
Sparse Core Ops, SparseCore 0:
  22.1 39.0 all-reduce.8
  88.3 52.2 all-reduce.4
  166.1 54.0 all-reduce.6
where the time goes:
time: 242 us; the launch traced here: 241 us
  waiting for transfers between devices  134 us (55%)
  other arithmetic  48.2 us (20%)
  matrix products  29.5 us (12%)
  between operations  13.9 us (6%)
  blocking collectives  11.6 us (5%)
  local copies, waits for them, and re-layouts  3.32 us (1%)
    psum x1, waiting for transfers between devices, shards(): gram_s = lax.psum(raw_gram(solved_c), 'gene')  52.1 us
    psum x1, waiting for transfers between devices, shards(): lax.psum(jnp.sum(partial_sum * context32[None, :, :], axis=1), 'gene')  43.1 us
    psum x1, waiting for transfers between devices, shards(): lax.psum((local_gram, jnp.sum(partial_sum * context32[:, None, :], axis=0...  39 us
    another operation x6, other arithmetic, solve_gram(): lower = jnp.linalg.cholesky(gram)  24.8 us
    another operation x4, other arithmetic, solve_gram(): lax.linalg.triangular_solve(lower, rhs, left_side=False, lower=True, tran...  20.9 us
    dot_general x1, matrix products, shards(): jnp.einsum('ikj,ir->kjr', tensor_block, pert_factor, preferred_element_ty...  13 us
    psum x1, blocking collectives, shards(): squares_a = lax.psum(jnp.sum(solved_a * solved_a, axis=0), 'pert')  11.6 us
    dot_general x1, matrix products, shards(): jnp.einsum('ikj,jr->ikr', tensor_block, gene_factor, preferred_element_ty...  9.45 us
  transfers between devices with their start and end apart: 3, of which 3 were waited for; matrix products, arithmetic and copies ran while one was open for 5% of the time, Pallas kernels for 0%

commit v1 on v0

v1 whole, which is shorter than its diff:
```python
import functools

import jax
import jax.numpy as jnp
from jax import lax
from jax.experimental import pallas as pl
from jax.experimental.pallas import tpu as pltpu
from jax.sharding import PartitionSpec as P

epsilon = 1e-06
MESH = pl.DeviceIdType.MESH
HIGHEST = lax.Precision.HIGHEST
PANEL = 8


def dot32(a, b, dims):
    return lax.dot_general(
        a, b, (dims, ((), ())), precision=HIGHEST, preferred_element_type=jnp.float32
    )


def invert_steps(a, steps):
    size = a.shape[0]
    lane = lax.broadcasted_iota(jnp.int32, (PANEL, size), 1)
    row = lax.broadcasted_iota(jnp.int32, (PANEL, size), 0)
    full_lane = lax.broadcasted_iota(jnp.int32, (size, size), 1)

    def step(_, a):
        panel = a[:PANEL]
        columns = [jnp.broadcast_to(panel[:, j : j + 1], (PANEL, size)) for j in range(PANEL)]
        for k in range(PANEL):
            inverse = 1.0 / columns[k][k : k + 1]
            pivot = jnp.where(lane[:1] == k, inverse, panel[k : k + 1] * inverse)
            kept = jnp.where(lane == k, 0.0, panel)
            panel = jnp.where(row == k, pivot, kept - columns[k] * pivot)
            for j in range(k + 1, PANEL):
                head = columns[j][k : k + 1] * inverse
                columns[j] = jnp.where(row == k, head, columns[j] - columns[k] * head)
        shift = size - PANEL
        turned = pltpu.roll(panel, shift, 1)
        rest = a[PANEL:]
        out = pltpu.roll(jnp.where(full_lane[PANEL:] < PANEL, 0.0, rest), shift, 1)
        for j in range(PANEL):
            out = out - rest[:, j : j + 1] * turned[j : j + 1]
        return jnp.concatenate([out, turned], axis=0)

    return lax.fori_loop(0, steps, step, a)


def sweep(
    n_pert, n_gene, tensor_hbm, factor_ref, context_ref, gene_ref, pert_ref,
    tensor, khatri, product, slab_send, gram_z, gram_g, matrix, mttkrp_part, mttkrp_in, mttkrp_all,
    second_part, second_in, squares_g, squares_z, final, load_sem,
    z_send, z_recv, g_send, g_recv,
):
    z = lax.axis_index("pert")
    g = lax.axis_index("gene")
    rows_i, rank = factor_ref.shape
    contexts = context_ref.shape[0]
    depth, rows_j = tensor.shape
    own_j = rows_j // n_pert
    own_i = rows_i // n_gene
    slab = rank // n_gene
    blocks, width = load_sem.shape[0], rows_j // load_sem.shape[0]
    per_block = width // own_j
    gene_count = rows_j * n_gene
    pert_count = rows_i * n_pert

    def z_copy(stage, src, dst, peer):
        return pltpu.make_async_remote_copy(
            src_ref=src, dst_ref=dst.at[z], send_sem=z_send.at[stage, peer],
            recv_sem=z_recv.at[stage, z], device_id=(peer, g), device_id_type=MESH,
        )

    def g_copy(stage, src, dst, peer):
        return pltpu.make_async_remote_copy(
            src_ref=src, dst_ref=dst.at[g], send_sem=g_send.at[stage, peer],
            recv_sem=g_recv.at[stage, g], device_id=(z, peer), device_id_type=MESH,
        )

    def z_wait(stage, dst):
        for d in range(1, n_pert):
            peer = lax.rem(z + d, n_pert)
            pltpu.make_async_remote_copy(
                src_ref=dst.at[peer], dst_ref=dst.at[peer], send_sem=z_send.at[stage, peer],
                recv_sem=z_recv.at[stage, peer], device_id=(peer, g), device_id_type=MESH,
            ).wait_recv()

    def g_wait(stage, dst):
        for d in range(1, n_gene):
            peer = lax.rem(g + d, n_gene)
            pltpu.make_async_remote_copy(
                src_ref=dst.at[peer], dst_ref=dst.at[peer], send_sem=g_send.at[stage, peer],
                recv_sem=g_recv.at[stage, peer], device_id=(z, peer), device_id_type=MESH,
            ).wait_recv()

    z_peers = [lax.rem(z + d, n_pert) for d in range(1, n_pert)]
    g_peers = [lax.rem(g + d, n_gene) for d in range(1, n_gene)]
    sent = []

    def send(copy):
        copy.start()
        sent.append(copy)

    barrier = pltpu.get_barrier_semaphore()
    for peer in z_peers:
        pl.semaphore_signal(barrier, inc=1, device_id=(peer, g), device_id_type=MESH)
    for peer in g_peers:
        pl.semaphore_signal(barrier, inc=1, device_id=(z, peer), device_id_type=MESH)

    def load(block):
        columns = pl.ds(pl.multiple_of(block * width, width), width)
        return pltpu.make_async_copy(
            tensor_hbm.at[:, columns], tensor.at[:, columns], load_sem.at[block]
        )

    order = [lax.rem(z // per_block + 1 + t, blocks) for t in range(blocks)]
    for block in order:
        load(block).start()

    factor = factor_ref[...]
    context = context_ref[...]
    context32 = context.astype(jnp.float32)
    gram_b = lax.dot_general(
        context, context, (((0,), (0,)), ((), ())), preferred_element_type=jnp.float32
    )
    gram = lax.dot_general(
        factor, factor, (((0,), (0,)), ((), ())), preferred_element_type=jnp.float32
    )
    for s in range(n_gene):
        slab_send[s] = gram[s * slab : (s + 1) * slab]
    pl.semaphore_wait(barrier, n_pert + n_gene - 2)

    gram_z[z] = slab_send[g]
    for peer in z_peers:
        send(z_copy(0, gram_z.at[z], gram_z, peer))

    step_i = 128

    def build(t, carry):
        part = factor_ref[pl.ds(pl.multiple_of(t * step_i, step_i), step_i), :]
        both = part.astype(jnp.float32)[:, None, :] * context32[None]
        both = both.reshape(step_i * contexts, rank)
        high = both.astype(jnp.bfloat16)
        low = (both - high.astype(jnp.float32)).astype(jnp.bfloat16)
        here = pl.ds(pl.multiple_of(t * step_i * contexts, step_i * contexts), step_i * contexts)
        khatri[here, :rank] = high
        khatri[here, rank:] = low
        return carry

    lax.fori_loop(0, rows_i // step_i, build, 0)

    z_wait(0, gram_z)
    total = gram_z[0]
    for s in range(1, n_pert):
        total = total + gram_z[s]
    gram_g[g] = total
    for peer in g_peers:
        send(g_copy(0, gram_g.at[g], gram_g, peer))

    step_d = 2048
    for t, block in enumerate(order):
        load(block).wait()
        columns = pl.ds(pl.multiple_of(block * width, width), width)
        product[...] = jnp.zeros_like(product)

        def multiply(c, carry):
            here = pl.ds(pl.multiple_of(c * step_d, step_d), step_d)
            product[...] += lax.dot_general(
                khatri[here, :], tensor[here, columns], (((0,), (0,)), ((), ())),
                preferred_element_type=jnp.float32,
            )
            return carry

        lax.fori_loop(0, depth // step_d, multiply, 0)
        turned = (product[:rank] + product[rank:]).T
        for q in range(per_block):
            owner = block * per_block + q
            mttkrp_part[owner] = turned[q * own_j : (q + 1) * own_j]

            @pl.when(owner != z)
            def _():
                z_copy(1, mttkrp_part.at[owner], mttkrp_in, owner).start()

    mttkrp_in[z] = mttkrp_part[z]
    for peer in z_peers:
        sent.append(z_copy(1, mttkrp_part.at[peer], mttkrp_in, peer))

    g_wait(0, gram_g)
    for s in range(n_gene):
        matrix[s * slab : (s + 1) * slab, :] = gram_g[s]
    steps = rank // PANEL
    early = steps // 4
    inverse = invert_steps(matrix[...] * gram_b, early)

    z_wait(1, mttkrp_in)
    total = mttkrp_in[0]
    for s in range(1, n_pert):
        total = total + mttkrp_in[s]
    mttkrp_all[z] = total
    for peer in z_peers:
        send(z_copy(2, mttkrp_all.at[z], mttkrp_all, peer))

    inverse = invert_steps(inverse, steps - early)
    z_wait(2, mttkrp_all)
    solved = dot32(mttkrp_all[...].reshape(rows_j, rank), inverse, ((1,), (0,)))
    gram = dot32(solved, solved, ((0,), (0,)))
    for s in range(n_gene):
        second_gram = gram[s * slab : (s + 1) * slab]
        slab_send[s] = second_gram

    gram_in, gram_out = gram_g.at[n_gene : 2 * n_gene], gram_g.at[2 * n_gene : 3 * n_gene]
    gram_in[g] = slab_send[g]
    for peer in g_peers:
        send(g_copy(1, slab_send.at[peer], gram_in, peer))
    g_wait(1, gram_in)
    total = gram_in[0]
    for s in range(1, n_gene):
        total = total + gram_in[s]
    gram_out[g] = total
    for peer in g_peers:
        send(g_copy(2, gram_out.at[g], gram_out, peer))
    g_wait(2, gram_out)
    for s in range(n_gene):
        matrix[s * slab : (s + 1) * slab, :] = gram_out[s]
    gram_s = matrix[...]

    diagonal = lax.broadcasted_iota(jnp.int32, (rank, rank), 0) == lax.broadcasted_iota(
        jnp.int32, (rank, rank), 1
    )
    on_diagonal = jnp.where(diagonal, gram_s, 0.0)
    scale_row = jnp.sqrt(jnp.sum(on_diagonal, axis=0, keepdims=True) / gene_count + epsilon)
    scale_column = jnp.sqrt(jnp.sum(on_diagonal, axis=1, keepdims=True) / gene_count + epsilon)
    gene_factor = (solved / scale_row).astype(jnp.bfloat16)
    gene_ref[...] = gene_factor
    gram_pert_mode = gram_s / (scale_column * scale_row) * gram_b

    def second(peer):
        here = pl.ds(pl.multiple_of(peer * own_i * contexts, own_i * contexts), own_i * contexts)
        partial = jnp.dot(tensor[here, :], gene_ref[...], preferred_element_type=jnp.float32)
        return jnp.sum(partial.reshape(own_i, contexts, rank) * context32[None], axis=1)

    def second_step(t, carry):
        peer = lax.rem(g + 1 + t, n_gene)
        second_part[peer] = second(peer)
        g_copy(3, second_part.at[peer], second_in, peer).start()
        return carry

    lax.fori_loop(0, n_gene - 1, second_step, 0)
    second_in[g] = second(g)
    for peer in g_peers:
        sent.append(g_copy(3, second_part.at[peer], second_in, peer))

    inverse = invert_steps(gram_pert_mode, steps)
    g_wait(3, second_in)
    total = second_in[0]
    for s in range(1, n_gene):
        total = total + second_in[s]
    solved = dot32(total, inverse, ((1,), (0,)))

    squares_g[g] = jnp.sum((solved * solved).reshape(own_i // 8, 8, rank), axis=0)
    for peer in g_peers:
        send(g_copy(4, squares_g.at[g], squares_g, peer))
    g_wait(4, squares_g)
    total = squares_g[0]
    for s in range(1, n_gene):
        total = total + squares_g[s]
    squares_z[z] = total
    for peer in z_peers:
        send(z_copy(3, squares_z.at[z], squares_z, peer))
    z_wait(3, squares_z)
    total = squares_z[0]
    for s in range(1, n_pert):
        total = total + squares_z[s]
    scale = jnp.sqrt(jnp.sum(total, axis=0, keepdims=True) / pert_count + epsilon)
    final[g] = (solved / scale).astype(jnp.bfloat16)
    for peer in g_peers:
        send(g_copy(5, final.at[g], final, peer))
    g_wait(5, final)
    for s in range(n_gene):
        pert_ref[s * own_i : (s + 1) * own_i, :] = final[s]
    for copy in sent:
        copy.wait_send()


def shards(n_pert, n_gene, tensor, pert_factor, context_factor):
    rows_i, contexts, rows_j = tensor.shape
    rank = pert_factor.shape[1]
    own_j, own_i, slab = rows_j // n_pert, rows_i // n_gene, rank // n_gene
    depth = rows_i * contexts
    width = 256
    f32, bf16 = jnp.float32, jnp.bfloat16
    vmem = pl.BlockSpec(memory_space=pltpu.VMEM)
    return pl.pallas_call(
        functools.partial(sweep, n_pert, n_gene),
        out_shape=(
            jax.ShapeDtypeStruct((rows_j, rank), bf16),
            jax.ShapeDtypeStruct((rows_i, rank), bf16),
        ),
        in_specs=[pl.BlockSpec(memory_space=pl.ANY), vmem, vmem],
        out_specs=(vmem, vmem),
        scratch_shapes=[
            pltpu.VMEM((depth, rows_j), bf16),
            pltpu.VMEM((depth, 2 * rank), bf16),
            pltpu.VMEM((2 * rank, width), f32),
            pltpu.VMEM((n_gene, slab, rank), f32),
            pltpu.VMEM((n_pert, slab, rank), f32),
            pltpu.VMEM((3 * n_gene, slab, rank), f32),
            pltpu.VMEM((rank, rank), f32),
            pltpu.VMEM((n_pert, own_j, rank), f32),
            pltpu.VMEM((n_pert, own_j, rank), f32),
            pltpu.VMEM((n_pert, own_j, rank), f32),
            pltpu.VMEM((n_gene, own_i, rank), f32),
            pltpu.VMEM((n_gene, own_i, rank), f32),
            pltpu.VMEM((n_gene, 8, rank), f32),
            pltpu.VMEM((n_pert, 8, rank), f32),
            pltpu.VMEM((n_gene, own_i, rank), bf16),
            pltpu.SemaphoreType.DMA((rows_j // width,)),
            pltpu.SemaphoreType.DMA((4, n_pert)),
            pltpu.SemaphoreType.DMA((4, n_pert)),
            pltpu.SemaphoreType.DMA((6, n_gene)),
            pltpu.SemaphoreType.DMA((6, n_gene)),
        ],
        compiler_params=pltpu.CompilerParams(
            collective_id=0, has_side_effects=True, vmem_limit_bytes=48 * 1024 * 1024
        ),
        name="sweep",
    )(tensor.reshape(depth, rows_j), pert_factor, context_factor)


def solution(mesh):
    return jax.shard_map(
        functools.partial(shards, mesh.shape["pert"], mesh.shape["gene"]),
        mesh=mesh,
        in_specs=(P("pert", None, "gene"), P("pert", None), P()),
        out_specs=(P("gene", None), P("pert", None)),
        check_vma=False,
    )
```

time: 242 us -> 56.2 us (0.23)
  waiting for transfers between devices: 134 us -> 0 us
  Pallas kernels: 0 us -> 52.4 us
  other arithmetic: 48.2 us -> 0 us
  matrix products: 29.5 us -> 0 us
  between operations: 13.9 us -> 0.65 us
  blocking collectives: 11.6 us -> 0 us
    psum x3 -> x0, waiting for transfers between devices: 134 us -> none  [the longest x1 52.1 us: shards(): gram_s = lax.psum(raw_gram(solved_c), 'gene')]
    pallas_call x0 -> x1, Pallas kernels: none -> 52.4 us  [shards(): pl.pallas_call(functools.partial(sweep, n_pert, n_gene), out_shape=(jax.S...]
    another operation x10 -> x0, other arithmetic: 45.7 us -> none  [the longest x6 24.8 us: solve_gram(): lower = jnp.linalg.cholesky(gram)]
    dot_general x5 -> x0, matrix products: 25.6 us -> none  [the longest x1 13 us: shards(): jnp.einsum('ikj,ir->kjr', tensor_block, pert_factor, preferred_element_ty...]
    psum x1 -> x0, blocking collectives: 11.6 us -> none  [shards(): squares_a = lax.psum(jnp.sum(solved_a * solved_a, axis=0), 'pert')]
    another operation x4 -> x0, matrix products: 3.89 us -> none  [the longest x2 2.91 us: solve_gram(): lax.linalg.triangular_solve(lower, rhs, left_side=False, lower=True, tran...]
  transfers between devices with their start and end apart: 3 -> 0, of which waited for: 3 -> 0; matrix products, arithmetic and copies ran while one was open for 5% -> 0% of each run, Pallas kernels for 0% -> 0%
where the time goes in v1:
time: 56.2 us; the launch traced here: 56.1 us
  Pallas kernels  52.4 us (93%)
  local copies, waits for them, and re-layouts  2.98 us (5%)
  between operations  0.65 us (1%)
    pallas_call x1, Pallas kernels, shards(): pl.pallas_call(functools.partial(sweep, n_pert, n_gene), out_shape=(jax.S...  52.4 us
    unnamed x6, local copies, waits for them, and re-layouts  2.98 us

profile of v1, /device:TPU:0, one launch (start us, length us, event | category | flops | bytes accessed | tf_op | source)
XLA Modules:
  0.0 56.1 jit_solution(388254091396358678)
XLA Ops:
  0.6 0.0 copy-start
  0.6 0.9 %copy-done = bf16[1024,128]{1,0:T(8,128)(2,1)S(1)} copy-done((bf16[1024,128]{1,0:T(8,128)(2,1)S(1)}, bf16[1024,128]{1,0:T(8,128)(2,1)}, u32[]{:S(2)}) %copy-start) | copy-done | bytes 262168
  1.6 0.0 copy-start.1
  1.6 0.7 %copy-done.1 = bf16[8,128]{1,0:T(8,128)(2,1)S(1)} copy-done((bf16[8,128]{1,0:T(8,128)(2,1)S(1)}, bf16[8,128]{1,0:T(8,128)(2,1)}, u32[]{:S(2)}) %copy-start.1) | copy-done | bytes 2072
  2.3 52.4 %sweep.1 = (bf16[512,128]{1,0:T(8,128)(2,1)S(1)}, bf16[1024,128]{1,0:T(8,128)(2,1)S(1)}) custom-call(bf16[8192,512]{1,0:T(8,128)(2,1)} %bitcast.1, bf16[1024,128]{1,0:T(8,128)(2,1)S(1)} %copy-done, bf16[8,128]{1,0:T(8,128)(2,1)S(1)} %copy-done.1), custom_call_target="tpu_custom_call" | custom-call | tf_op jit(solution)/shard_map/sweep/pallas_call | solution.py:294
  54.7 0.7 %copy.7 = bf16[512,128]{1,0:T(8,128)(2,1)} copy(bf16[512,128]{1,0:T(8,128)(2,1)S(1)} %get-tuple-element.4) | data formatting | bytes 262144
  55.4 0.7 %copy.8 = bf16[1024,128]{1,0:T(8,128)(2,1)} copy(bf16[1024,128]{1,0:T(8,128)(2,1)S(1)} %get-tuple-element.5) | data formatting | bytes 524288
Async XLA Ops:
  0.6 1.0 %copy-start = (bf16[1024,128]{1,0:T(8,128)(2,1)S(1)}, bf16[1024,128]{1,0:T(8,128)(2,1)}, u32[]{:S(2)}) copy-start(bf16[1024,128]{1,0:T(8,128)(2,1)} %factor_ref.1) | copy-start | bytes 786436
  1.6 0.7 %copy-start.1 = (bf16[8,128]{1,0:T(8,128)(2,1)S(1)}, bf16[8,128]{1,0:T(8,128)(2,1)}, u32[]{:S(2)}) copy-start(bf16[8,128]{1,0:T(8,128)(2,1)} %context_ref.1) | copy-start | bytes 6148

commit v2 on v1

--- a/solution.py
+++ b/solution.py
@@ -19,38 +19,45 @@
     )
 
 
-def invert_steps(a, steps):
+def reciprocal(x):
+    r = pl.reciprocal(x, approx=True)
+    r = r * (2.0 - x * r)
+    return r * (2.0 - x * r)
+
+
+def invert_step(a):
     size = a.shape[0]
     lane = lax.broadcasted_iota(jnp.int32, (PANEL, size), 1)
     row = lax.broadcasted_iota(jnp.int32, (PANEL, size), 0)
-    full_lane = lax.broadcasted_iota(jnp.int32, (size, size), 1)
-
-    def step(_, a):
-        panel = a[:PANEL]
-        columns = [jnp.broadcast_to(panel[:, j : j + 1], (PANEL, size)) for j in range(PANEL)]
-        for k in range(PANEL):
-            inverse = 1.0 / columns[k][k : k + 1]
-            pivot = jnp.where(lane[:1] == k, inverse, panel[k : k + 1] * inverse)
-            kept = jnp.where(lane == k, 0.0, panel)
-            panel = jnp.where(row == k, pivot, kept - columns[k] * pivot)
-            for j in range(k + 1, PANEL):
-                head = columns[j][k : k + 1] * inverse
-                columns[j] = jnp.where(row == k, head, columns[j] - columns[k] * head)
-        shift = size - PANEL
-        turned = pltpu.roll(panel, shift, 1)
-        rest = a[PANEL:]
-        out = pltpu.roll(jnp.where(full_lane[PANEL:] < PANEL, 0.0, rest), shift, 1)
-        for j in range(PANEL):
-            out = out - rest[:, j : j + 1] * turned[j : j + 1]
-        return jnp.concatenate([out, turned], axis=0)
-
-    return lax.fori_loop(0, steps, step, a)
+    rest_lane = lax.broadcasted_iota(jnp.int32, (size - PANEL, size), 1)
+    panel = a[:PANEL]
+    columns = [jnp.broadcast_to(panel[:, j : j + 1], (PANEL, size)) for j in range(PANEL)]
+    for k in range(PANEL):
+        inverse = reciprocal(columns[k][k : k + 1])
+        pivot = jnp.where(lane[k : k + 1] == k, inverse, panel[k : k + 1] * inverse)
+        kept = jnp.where(lane == k, 0.0, panel)
+        panel = jnp.where(row == k, pivot, kept - columns[k] * pivot)
+        for j in range(k + 1, PANEL):
+            head = columns[j][k : k + 1] * inverse
+            columns[j] = jnp.where(row == k, head, columns[j] - columns[k] * head)
+    shift = size - PANEL
+    turned = pltpu.roll(panel, shift, 1)
+    rest = a[PANEL:]
+    out = pltpu.roll(jnp.where(rest_lane < PANEL, 0.0, rest), shift, 1)
+    for j in range(PANEL):
+        out = out - rest[:, j : j + 1] * turned[j : j + 1]
+    return jnp.concatenate([out, turned], axis=0)
+
+
+def invert_steps(a, steps):
+    return lax.fori_loop(0, steps, lambda _, a: invert_step(a), a)
 
 
 def sweep(
-    n_pert, n_gene, tensor_hbm, factor_ref, context_ref, gene_ref, pert_ref,
-    tensor, khatri, product, slab_send, gram_z, gram_g, matrix, mttkrp_part, mttkrp_in, mttkrp_all,
-    second_part, second_in, squares_g, squares_z, final, load_sem,
+    n_pert, n_gene, tensor_hbm, factor_hbm, context_hbm, gene_ref, pert_ref,
+    factor_ref, context_ref, tensor, khatri, product, slab_send, gram_z, gram_g, matrix,
+    mttkrp_part, mttkrp_in, gene_all,
+    second_part, second_in, squares_g, squares_z, final, load_sem, small_sem,
     z_send, z_recv, g_send, g_recv,
 ):
     z = lax.axis_index("pert")
@@ -115,8 +122,16 @@
         )
 
     order = [lax.rem(z // per_block + 1 + t, blocks) for t in range(blocks)]
+    small = [
+        pltpu.make_async_copy(factor_hbm, factor_ref, small_sem.at[0]),
+        pltpu.make_async_copy(context_hbm, context_ref, small_sem.at[1]),
+    ]
+    for copy in small:
+        copy.start()
     for block in order:
         load(block).start()
+    for copy in small:
+        copy.wait()
 
     factor = factor_ref[...]
     context = context_ref[...]
@@ -136,19 +151,29 @@
         send(z_copy(0, gram_z.at[z], gram_z, peer))
 
     step_i = 128
-
-    def build(t, carry):
-        part = factor_ref[pl.ds(pl.multiple_of(t * step_i, step_i), step_i), :]
-        both = part.astype(jnp.float32)[:, None, :] * context32[None]
-        both = both.reshape(step_i * contexts, rank)
+    step_p = step_i * contexts
+    repeat = (
+        lax.broadcasted_iota(jnp.int32, (step_i, step_p), 1) // contexts
+        == lax.broadcasted_iota(jnp.int32, (step_i, step_p), 0)
+    ).astype(jnp.bfloat16)
+    cycle = (
+        lax.rem(lax.broadcasted_iota(jnp.int32, (contexts, step_p), 1), contexts)
+        == lax.broadcasted_iota(jnp.int32, (contexts, step_p), 0)
+    ).astype(jnp.bfloat16)
+    context_rows = lax.dot_general(
+        context, cycle, (((0,), (0,)), ((), ())), preferred_element_type=jnp.float32
+    )
+
+    for t in range(rows_i // step_i):
+        both = context_rows * lax.dot_general(
+            factor_ref[t * step_i : (t + 1) * step_i, :], repeat, (((0,), (0,)), ((), ())),
+            preferred_element_type=jnp.float32,
+        )
         high = both.astype(jnp.bfloat16)
-        low = (both - high.astype(jnp.float32)).astype(jnp.bfloat16)
-        here = pl.ds(pl.multiple_of(t * step_i * contexts, step_i * contexts), step_i * contexts)
-        khatri[here, :rank] = high
-        khatri[here, rank:] = low
-        return carry
-
-    lax.fori_loop(0, rows_i // step_i, build, 0)
+        khatri[:rank, t * step_p : (t + 1) * step_p] = high
+        khatri[rank:, t * step_p : (t + 1) * step_p] = (
+            both - high.astype(jnp.float32)
+        ).astype(jnp.bfloat16)
 
     z_wait(0, gram_z)
     total = gram_z[0]
@@ -159,20 +184,34 @@
         send(g_copy(0, gram_g.at[g], gram_g, peer))
 
     step_d = 2048
+    chunks = depth // step_d
+    steps = rank // PANEL
+    early = min(2, steps // chunks)
+
+    def multiply(c, columns):
+        here = pl.ds(pl.multiple_of(c * step_d, step_d), step_d)
+        product[...] += jnp.dot(
+            khatri[:, here], tensor[here, columns], preferred_element_type=jnp.float32
+        )
+
     for t, block in enumerate(order):
         load(block).wait()
         columns = pl.ds(pl.multiple_of(block * width, width), width)
         product[...] = jnp.zeros_like(product)
-
-        def multiply(c, carry):
-            here = pl.ds(pl.multiple_of(c * step_d, step_d), step_d)
-            product[...] += lax.dot_general(
-                khatri[here, :], tensor[here, columns], (((0,), (0,)), ((), ())),
-                preferred_element_type=jnp.float32,
-            )
-            return carry
-
-        lax.fori_loop(0, depth // step_d, multiply, 0)
+        if t < blocks - 1:
+            lax.fori_loop(0, chunks, lambda c, carry: (multiply(c, columns), carry)[1], 0)
+        else:
+            g_wait(0, gram_g)
+            for s in range(n_gene):
+                matrix[s * slab : (s + 1) * slab, :] = gram_g[s]
+
+            def both_steps(c, inverse):
+                multiply(c, columns)
+                for _ in range(early):
+                    inverse = invert_step(inverse)
+                return inverse
+
+            inverse = lax.fori_loop(0, chunks, both_steps, matrix[...] * gram_b)
         turned = (product[:rank] + product[rank:]).T
         for q in range(per_block):
             owner = block * per_block + q
@@ -186,28 +225,15 @@
     for peer in z_peers:
         sent.append(z_copy(1, mttkrp_part.at[peer], mttkrp_in, peer))
 
-    g_wait(0, gram_g)
-    for s in range(n_gene):
-        matrix[s * slab : (s + 1) * slab, :] = gram_g[s]
-    steps = rank // PANEL
-    early = steps // 4
-    inverse = invert_steps(matrix[...] * gram_b, early)
-
+    inverse = invert_steps(inverse, steps - early * chunks)
     z_wait(1, mttkrp_in)
     total = mttkrp_in[0]
     for s in range(1, n_pert):
         total = total + mttkrp_in[s]
-    mttkrp_all[z] = total
-    for peer in z_peers:
-        send(z_copy(2, mttkrp_all.at[z], mttkrp_all, peer))
-
-    inverse = invert_steps(inverse, steps - early)
-    z_wait(2, mttkrp_all)
-    solved = dot32(mttkrp_all[...].reshape(rows_j, rank), inverse, ((1,), (0,)))
+    solved = dot32(total, inverse, ((1,), (0,)))
     gram = dot32(solved, solved, ((0,), (0,)))
     for s in range(n_gene):
-        second_gram = gram[s * slab : (s + 1) * slab]
-        slab_send[s] = second_gram
+        slab_send[s] = gram[s * slab : (s + 1) * slab]
 
     gram_in, gram_out = gram_g.at[n_gene : 2 * n_gene], gram_g.at[2 * n_gene : 3 * n_gene]
     gram_in[g] = slab_send[g]
@@ -217,6 +243,14 @@
     total = gram_in[0]
     for s in range(1, n_gene):
         total = total + gram_in[s]
+    slab_z = gram_z.at[n_pert : 2 * n_pert]
+    slab_z[z] = total
+    for peer in z_peers:
+        send(z_copy(2, slab_z.at[z], slab_z, peer))
+    z_wait(2, slab_z)
+    total = slab_z[0]
+    for s in range(1, n_pert):
+        total = total + slab_z[s]
     gram_out[g] = total
     for peer in g_peers:
         send(g_copy(2, gram_out.at[g], gram_out, peer))
@@ -231,27 +265,35 @@
     on_diagonal = jnp.where(diagonal, gram_s, 0.0)
     scale_row = jnp.sqrt(jnp.sum(on_diagonal, axis=0, keepdims=True) / gene_count + epsilon)
     scale_column = jnp.sqrt(jnp.sum(on_diagonal, axis=1, keepdims=True) / gene_count + epsilon)
-    gene_factor = (solved / scale_row).astype(jnp.bfloat16)
-    gene_ref[...] = gene_factor
+    gene_all[z] = (solved / scale_row).astype(jnp.bfloat16)
+    for peer in z_peers:
+        send(z_copy(4, gene_all.at[z], gene_all, peer))
     gram_pert_mode = gram_s / (scale_column * scale_row) * gram_b
+
+    z_wait(4, gene_all)
+    for s in range(n_pert):
+        gene_ref[s * own_j : (s + 1) * own_j, :] = gene_all[s]
 
     def second(peer):
         here = pl.ds(pl.multiple_of(peer * own_i * contexts, own_i * contexts), own_i * contexts)
         partial = jnp.dot(tensor[here, :], gene_ref[...], preferred_element_type=jnp.float32)
         return jnp.sum(partial.reshape(own_i, contexts, rank) * context32[None], axis=1)
 
-    def second_step(t, carry):
+    beside = steps // n_gene
+
+    def second_step(t, inverse):
         peer = lax.rem(g + 1 + t, n_gene)
         second_part[peer] = second(peer)
         g_copy(3, second_part.at[peer], second_in, peer).start()
-        return carry
-
-    lax.fori_loop(0, n_gene - 1, second_step, 0)
+        for _ in range(beside):
+            inverse = invert_step(inverse)
+        return inverse
+
+    inverse = lax.fori_loop(0, n_gene - 1, second_step, gram_pert_mode)
     second_in[g] = second(g)
     for peer in g_peers:
         sent.append(g_copy(3, second_part.at[peer], second_in, peer))
-
-    inverse = invert_steps(gram_pert_mode, steps)
+    inverse = invert_steps(inverse, steps - beside * (n_gene - 1))
     g_wait(3, second_in)
     total = second_in[0]
     for s in range(1, n_gene):
@@ -297,32 +339,35 @@
             jax.ShapeDtypeStruct((rows_j, rank), bf16),
             jax.ShapeDtypeStruct((rows_i, rank), bf16),
         ),
-        in_specs=[pl.BlockSpec(memory_space=pl.ANY), vmem, vmem],
+        in_specs=[pl.BlockSpec(memory_space=pl.ANY)] * 3,
         out_specs=(vmem, vmem),
         scratch_shapes=[
+            pltpu.VMEM((rows_i, rank), bf16),
+            pltpu.VMEM((contexts, rank), bf16),
             pltpu.VMEM((depth, rows_j), bf16),
-            pltpu.VMEM((depth, 2 * rank), bf16),
+            pltpu.VMEM((2 * rank, depth), bf16),
             pltpu.VMEM((2 * rank, width), f32),
             pltpu.VMEM((n_gene, slab, rank), f32),
-            pltpu.VMEM((n_pert, slab, rank), f32),
+            pltpu.VMEM((2 * n_pert, slab, rank), f32),
             pltpu.VMEM((3 * n_gene, slab, rank), f32),
             pltpu.VMEM((rank, rank), f32),
             pltpu.VMEM((n_pert, own_j, rank), f32),
             pltpu.VMEM((n_pert, own_j, rank), f32),
-            pltpu.VMEM((n_pert, own_j, rank), f32),
+            pltpu.VMEM((n_pert, own_j, rank), bf16),
             pltpu.VMEM((n_gene, own_i, rank), f32),
             pltpu.VMEM((n_gene, own_i, rank), f32),
             pltpu.VMEM((n_gene, 8, rank), f32),
             pltpu.VMEM((n_pert, 8, rank), f32),
             pltpu.VMEM((n_gene, own_i, rank), bf16),
             pltpu.SemaphoreType.DMA((rows_j // width,)),
-            pltpu.SemaphoreType.DMA((4, n_pert)),
-            pltpu.SemaphoreType.DMA((4, n_pert)),
+            pltpu.SemaphoreType.DMA((2,)),
+            pltpu.SemaphoreType.DMA((5, n_pert)),
+            pltpu.SemaphoreType.DMA((5, n_pert)),
             pltpu.SemaphoreType.DMA((6, n_gene)),
             pltpu.SemaphoreType.DMA((6, n_gene)),
         ],
         compiler_params=pltpu.CompilerParams(
-            collective_id=0, has_side_effects=True, vmem_limit_bytes=48 * 1024 * 1024
+            collective_id=0, has_side_effects=True, vmem_limit_bytes=64 * 1024 * 1024 - 65536
         ),
         name="sweep",
     )(tensor.reshape(depth, rows_j), pert_factor, context_factor)

time: 56.2 us -> 59.5 us (1.059)
  Pallas kernels: 52.4 us -> 55.5 us
    pallas_call x1, Pallas kernels: 52.4 us -> 55.5 us  [shards(): pl.pallas_call(functools.partial(sweep, n_pert, n_gene), out_shape=(jax.S...]
    unnamed x6 -> x2, local copies, waits for them, and re-layouts: 2.98 us -> 3.24 us
where the time goes in v2:
time: 59.5 us; the launch traced here: 59.3 us
  Pallas kernels  55.5 us (93%)
  local copies, waits for them, and re-layouts  3.24 us (5%)
  between operations  0.64 us (1%)
    pallas_call x1, Pallas kernels, shards(): pl.pallas_call(functools.partial(sweep, n_pert, n_gene), out_shape=(jax.S...  55.5 us
    unnamed x2, local copies, waits for them, and re-layouts  3.24 us

profile of v2, /device:TPU:0, one launch (start us, length us, event | category | flops | bytes accessed | tf_op | source)
XLA Modules:
  0.0 59.3 jit_solution(13401000533104559617)
XLA Ops:
  0.6 55.5 %sweep.1 = (bf16[512,128]{1,0:T(8,128)(2,1)}, bf16[1024,128]{1,0:T(8,128)(2,1)}) custom-call(bf16[8192,512]{1,0:T(8,128)(2,1)} %bitcast.1, bf16[1024,128]{1,0:T(8,128)(2,1)} %factor_hbm.1, bf16[8,128]{1,0:T(8,128)(2,1)} %context_hbm.1), custom_call_target="tpu_custom_call" | custom-call | tf_op jit(solution)/shard_map/sweep/pallas_call | solution.py:336
  56.1 1.6 %copy.7 = bf16[512,128]{1,0:T(8,128)(2,1)} copy(bf16[512,128]{1,0:T(8,128)(2,1)} %get-tuple-element.4) | data formatting | bytes 262144
  57.7 1.7 %copy.8 = bf16[1024,128]{1,0:T(8,128)(2,1)} copy(bf16[1024,128]{1,0:T(8,128)(2,1)} %get-tuple-element.5) | data formatting | bytes 524288

commit v3 on v2

--- a/solution.py
+++ b/solution.py
@@ -54,10 +54,10 @@
 
 
 def sweep(
-    n_pert, n_gene, tensor_hbm, factor_hbm, context_hbm, gene_ref, pert_ref,
-    factor_ref, context_ref, tensor, khatri, product, slab_send, gram_z, gram_g, matrix,
-    mttkrp_part, mttkrp_in, gene_all,
-    second_part, second_in, squares_g, squares_z, final, load_sem, small_sem,
+    n_pert, n_gene, tensor_hbm, factor_ref, context_ref, gene_ref, pert_ref,
+    tensor, khatri, product, slab_send, gram_z, gram_g, matrix,
+    mttkrp_part, mttkrp_in, mttkrp_all,
+    second_part, second_in, squares_g, squares_z, final, load_sem,
     z_send, z_recv, g_send, g_recv,
 ):
     z = lax.axis_index("pert")
@@ -122,16 +122,8 @@
         )
 
     order = [lax.rem(z // per_block + 1 + t, blocks) for t in range(blocks)]
-    small = [
-        pltpu.make_async_copy(factor_hbm, factor_ref, small_sem.at[0]),
-        pltpu.make_async_copy(context_hbm, context_ref, small_sem.at[1]),
-    ]
-    for copy in small:
-        copy.start()
     for block in order:
         load(block).start()
-    for copy in small:
-        copy.wait()
 
     factor = factor_ref[...]
     context = context_ref[...]
@@ -225,28 +217,33 @@
     for peer in z_peers:
         sent.append(z_copy(1, mttkrp_part.at[peer], mttkrp_in, peer))
 
-    inverse = invert_steps(inverse, steps - early * chunks)
+    left = steps - early * chunks
+    tail = left // 4
+    inverse = invert_steps(inverse, left - 2 * tail)
     z_wait(1, mttkrp_in)
     total = mttkrp_in[0]
     for s in range(1, n_pert):
         total = total + mttkrp_in[s]
-    solved = dot32(total, inverse, ((1,), (0,)))
-    gram = dot32(solved, solved, ((0,), (0,)))
+    mttkrp_all[z] = total
+    gram = dot32(total, total, ((0,), (0,)))
     for s in range(n_gene):
         slab_send[s] = gram[s * slab : (s + 1) * slab]
-
     gram_in, gram_out = gram_g.at[n_gene : 2 * n_gene], gram_g.at[2 * n_gene : 3 * n_gene]
+    slab_z = gram_z.at[n_pert : 2 * n_pert]
     gram_in[g] = slab_send[g]
     for peer in g_peers:
         send(g_copy(1, slab_send.at[peer], gram_in, peer))
+    for peer in z_peers:
+        send(z_copy(4, mttkrp_all.at[z], mttkrp_all, peer))
+    inverse = invert_steps(inverse, tail)
     g_wait(1, gram_in)
     total = gram_in[0]
     for s in range(1, n_gene):
         total = total + gram_in[s]
-    slab_z = gram_z.at[n_pert : 2 * n_pert]
     slab_z[z] = total
     for peer in z_peers:
         send(z_copy(2, slab_z.at[z], slab_z, peer))
+    inverse = invert_steps(inverse, tail)
     z_wait(2, slab_z)
     total = slab_z[0]
     for s in range(1, n_pert):
@@ -254,10 +251,12 @@
     gram_out[g] = total
     for peer in g_peers:
         send(g_copy(2, gram_out.at[g], gram_out, peer))
+    z_wait(4, mttkrp_all)
+    solved = dot32(mttkrp_all[...].reshape(rows_j, rank), inverse, ((1,), (0,)))
     g_wait(2, gram_out)
     for s in range(n_gene):
         matrix[s * slab : (s + 1) * slab, :] = gram_out[s]
-    gram_s = matrix[...]
+    gram_s = dot32(dot32(inverse, matrix[...], ((0,), (0,))), inverse, ((1,), (0,)))
 
     diagonal = lax.broadcasted_iota(jnp.int32, (rank, rank), 0) == lax.broadcasted_iota(
         jnp.int32, (rank, rank), 1
@@ -265,14 +264,8 @@
     on_diagonal = jnp.where(diagonal, gram_s, 0.0)
     scale_row = jnp.sqrt(jnp.sum(on_diagonal, axis=0, keepdims=True) / gene_count + epsilon)
     scale_column = jnp.sqrt(jnp.sum(on_diagonal, axis=1, keepdims=True) / gene_count + epsilon)
-    gene_all[z] = (solved / scale_row).astype(jnp.bfloat16)
-    for peer in z_peers:
-        send(z_copy(4, gene_all.at[z], gene_all, peer))
+    gene_ref[...] = (solved / scale_row).astype(jnp.bfloat16)
     gram_pert_mode = gram_s / (scale_column * scale_row) * gram_b
-
-    z_wait(4, gene_all)
-    for s in range(n_pert):
-        gene_ref[s * own_j : (s + 1) * own_j, :] = gene_all[s]
 
     def second(peer):
         here = pl.ds(pl.multiple_of(peer * own_i * contexts, own_i * contexts), own_i * contexts)
@@ -303,6 +296,9 @@
     squares_g[g] = jnp.sum((solved * solved).reshape(own_i // 8, 8, rank), axis=0)
     for peer in g_peers:
         send(g_copy(4, squares_g.at[g], squares_g, peer))
+    final[g] = solved
+    for peer in g_peers:
+        send(g_copy(5, final.at[g], final, peer))
     g_wait(4, squares_g)
     total = squares_g[0]
     for s in range(1, n_gene):
@@ -315,12 +311,9 @@
     for s in range(1, n_pert):
         total = total + squares_z[s]
     scale = jnp.sqrt(jnp.sum(total, axis=0, keepdims=True) / pert_count + epsilon)
-    final[g] = (solved / scale).astype(jnp.bfloat16)
-    for peer in g_peers:
-        send(g_copy(5, final.at[g], final, peer))
     g_wait(5, final)
     for s in range(n_gene):
-        pert_ref[s * own_i : (s + 1) * own_i, :] = final[s]
+        pert_ref[s * own_i : (s + 1) * own_i, :] = (final[s] / scale).astype(jnp.bfloat16)
     for copy in sent:
         copy.wait_send()
 
@@ -339,11 +332,9 @@
             jax.ShapeDtypeStruct((rows_j, rank), bf16),
             jax.ShapeDtypeStruct((rows_i, rank), bf16),
         ),
-        in_specs=[pl.BlockSpec(memory_space=pl.ANY)] * 3,
+        in_specs=[pl.BlockSpec(memory_space=pl.ANY), vmem, vmem],
         out_specs=(vmem, vmem),
         scratch_shapes=[
-            pltpu.VMEM((rows_i, rank), bf16),
-            pltpu.VMEM((contexts, rank), bf16),
             pltpu.VMEM((depth, rows_j), bf16),
             pltpu.VMEM((2 * rank, depth), bf16),
             pltpu.VMEM((2 * rank, width), f32),
@@ -353,21 +344,20 @@
             pltpu.VMEM((rank, rank), f32),
             pltpu.VMEM((n_pert, own_j, rank), f32),
             pltpu.VMEM((n_pert, own_j, rank), f32),
-            pltpu.VMEM((n_pert, own_j, rank), bf16),
+            pltpu.VMEM((n_pert, own_j, rank), f32),
             pltpu.VMEM((n_gene, own_i, rank), f32),
             pltpu.VMEM((n_gene, own_i, rank), f32),
             pltpu.VMEM((n_gene, 8, rank), f32),
             pltpu.VMEM((n_pert, 8, rank), f32),
-            pltpu.VMEM((n_gene, own_i, rank), bf16),
+            pltpu.VMEM((n_gene, own_i, rank), f32),
             pltpu.SemaphoreType.DMA((rows_j // width,)),
-            pltpu.SemaphoreType.DMA((2,)),
             pltpu.SemaphoreType.DMA((5, n_pert)),
             pltpu.SemaphoreType.DMA((5, n_pert)),
             pltpu.SemaphoreType.DMA((6, n_gene)),
             pltpu.SemaphoreType.DMA((6, n_gene)),
         ],
         compiler_params=pltpu.CompilerParams(
-            collective_id=0, has_side_effects=True, vmem_limit_bytes=64 * 1024 * 1024 - 65536
+            collective_id=0, has_side_effects=True, vmem_limit_bytes=48 * 1024 * 1024
         ),
         name="sweep",
     )(tensor.reshape(depth, rows_j), pert_factor, context_factor)

time: 59.5 us -> 53.7 us (0.903); the launches traced: 59.3 us -> 52.9 us
  Pallas kernels: 55.5 us -> 49.3 us
    pallas_call x1, Pallas kernels: 55.5 us -> 49.3 us  [shards(): pl.pallas_call(functools.partial(sweep, n_pert, n_gene), out_shape=(jax.S...]
    unnamed x2 -> x6, local copies, waits for them, and re-layouts: 3.24 us -> 2.98 us
where the time goes in v3:
time: 53.7 us; the launch traced here: 52.9 us
  Pallas kernels  49.3 us (92%)
  local copies, waits for them, and re-layouts  2.98 us (6%)
  between operations  0.65 us (1%)
    pallas_call x1, Pallas kernels, shards(): pl.pallas_call(functools.partial(sweep, n_pert, n_gene), out_shape=(jax.S...  49.3 us
    unnamed x6, local copies, waits for them, and re-layouts  2.98 us

profile of v3, /device:TPU:0, one launch (start us, length us, event | category | flops | bytes accessed | tf_op | source)
XLA Modules:
  0.0 52.9 jit_solution(14817003758311421654)
XLA Ops:
  0.6 0.0 copy-start
  0.6 0.9 %copy-done = bf16[1024,128]{1,0:T(8,128)(2,1)S(1)} copy-done((bf16[1024,128]{1,0:T(8,128)(2,1)S(1)}, bf16[1024,128]{1,0:T(8,128)(2,1)}, u32[]{:S(2)}) %copy-start) | copy-done | bytes 262168
  1.6 0.0 copy-start.1
  1.6 0.7 %copy-done.1 = bf16[8,128]{1,0:T(8,128)(2,1)S(1)} copy-done((bf16[8,128]{1,0:T(8,128)(2,1)S(1)}, bf16[8,128]{1,0:T(8,128)(2,1)}, u32[]{:S(2)}) %copy-start.1) | copy-done | bytes 2072
  2.3 49.3 %sweep.1 = (bf16[512,128]{1,0:T(8,128)(2,1)S(1)}, bf16[1024,128]{1,0:T(8,128)(2,1)S(1)}) custom-call(bf16[8192,512]{1,0:T(8,128)(2,1)} %bitcast.1, bf16[1024,128]{1,0:T(8,128)(2,1)S(1)} %copy-done, bf16[8,128]{1,0:T(8,128)(2,1)S(1)} %copy-done.1), custom_call_target="tpu_custom_call" | custom-call | tf_op jit(solution)/shard_map/sweep/pallas_call | solution.py:329
  51.5 0.7 %copy.7 = bf16[512,128]{1,0:T(8,128)(2,1)} copy(bf16[512,128]{1,0:T(8,128)(2,1)S(1)} %get-tuple-element.4) | data formatting | bytes 262144
  52.2 0.7 %copy.8 = bf16[1024,128]{1,0:T(8,128)(2,1)} copy(bf16[1024,128]{1,0:T(8,128)(2,1)S(1)} %get-tuple-element.5) | data formatting | bytes 524288
Async XLA Ops:
  0.6 1.0 %copy-start = (bf16[1024,128]{1,0:T(8,128)(2,1)S(1)}, bf16[1024,128]{1,0:T(8,128)(2,1)}, u32[]{:S(2)}) copy-start(bf16[1024,128]{1,0:T(8,128)(2,1)} %factor_ref.1) | copy-start | bytes 786436
  1.6 0.7 %copy-start.1 = (bf16[8,128]{1,0:T(8,128)(2,1)S(1)}, bf16[8,128]{1,0:T(8,128)(2,1)}, u32[]{:S(2)}) copy-start(bf16[8,128]{1,0:T(8,128)(2,1)} %context_ref.1) | copy-start | bytes 6148

commit v4 on v3

--- a/solution.py
+++ b/solution.py
@@ -267,10 +267,22 @@
     gene_ref[...] = (solved / scale_row).astype(jnp.bfloat16)
     gram_pert_mode = gram_s / (scale_column * scale_row) * gram_b
 
+    add_contexts = (
+        lax.broadcasted_iota(jnp.int32, (own_i, own_i * contexts), 1) // contexts
+        == lax.broadcasted_iota(jnp.int32, (own_i, own_i * contexts), 0)
+    ).astype(jnp.bfloat16)
+
     def second(peer):
         here = pl.ds(pl.multiple_of(peer * own_i * contexts, own_i * contexts), own_i * contexts)
         partial = jnp.dot(tensor[here, :], gene_ref[...], preferred_element_type=jnp.float32)
-        return jnp.sum(partial.reshape(own_i, contexts, rank) * context32[None], axis=1)
+        terms = partial.reshape(own_i, contexts, rank) * context32[None]
+        terms = terms.reshape(own_i * contexts, rank)
+        high = terms.astype(jnp.bfloat16)
+        low = (terms - high.astype(jnp.float32)).astype(jnp.bfloat16)
+        both = jnp.dot(
+            add_contexts, jnp.concatenate([high, low], axis=1), preferred_element_type=jnp.float32
+        )
+        return both[:, :rank] + both[:, rank:]
 
     beside = steps // n_gene
 

time: 53.7 us -> 53.7 us (level)
  no operation moved by 1% of the time
where the time goes in v4:
time: 53.7 us; the launch traced here: 52.9 us
  Pallas kernels  49.3 us (92%)
  local copies, waits for them, and re-layouts  2.98 us (6%)
  between operations  0.65 us (1%)
    pallas_call x1, Pallas kernels, shards(): pl.pallas_call(functools.partial(sweep, n_pert, n_gene), out_shape=(jax.S...  49.3 us
    unnamed x6, local copies, waits for them, and re-layouts  2.98 us

profile of v4, /device:TPU:0, one launch (start us, length us, event | category | flops | bytes accessed | tf_op | source)
XLA Modules:
  0.0 52.9 jit_solution(1497485825491815045)
XLA Ops:
  0.6 0.0 copy-start
  0.6 0.9 %copy-done = bf16[1024,128]{1,0:T(8,128)(2,1)S(1)} copy-done((bf16[1024,128]{1,0:T(8,128)(2,1)S(1)}, bf16[1024,128]{1,0:T(8,128)(2,1)}, u32[]{:S(2)}) %copy-start) | copy-done | bytes 262168
  1.6 0.0 copy-start.1
  1.6 0.7 %copy-done.1 = bf16[8,128]{1,0:T(8,128)(2,1)S(1)} copy-done((bf16[8,128]{1,0:T(8,128)(2,1)S(1)}, bf16[8,128]{1,0:T(8,128)(2,1)}, u32[]{:S(2)}) %copy-start.1) | copy-done | bytes 2072
  2.3 49.3 %sweep.1 = (bf16[512,128]{1,0:T(8,128)(2,1)S(1)}, bf16[1024,128]{1,0:T(8,128)(2,1)S(1)}) custom-call(bf16[8192,512]{1,0:T(8,128)(2,1)} %bitcast.1, bf16[1024,128]{1,0:T(8,128)(2,1)S(1)} %copy-done, bf16[8,128]{1,0:T(8,128)(2,1)S(1)} %copy-done.1), custom_call_target="tpu_custom_call" | custom-call | tf_op jit(solution)/shard_map/sweep/pallas_call | solution.py:341
  51.5 0.7 %copy.7 = bf16[512,128]{1,0:T(8,128)(2,1)} copy(bf16[512,128]{1,0:T(8,128)(2,1)S(1)} %get-tuple-element.4) | data formatting | bytes 262144
  52.2 0.7 %copy.8 = bf16[1024,128]{1,0:T(8,128)(2,1)} copy(bf16[1024,128]{1,0:T(8,128)(2,1)S(1)} %get-tuple-element.5) | data formatting | bytes 524288
Async XLA Ops:
  0.6 1.0 %copy-start = (bf16[1024,128]{1,0:T(8,128)(2,1)S(1)}, bf16[1024,128]{1,0:T(8,128)(2,1)}, u32[]{:S(2)}) copy-start(bf16[1024,128]{1,0:T(8,128)(2,1)} %factor_ref.1) | copy-start | bytes 786436
  1.6 0.7 %copy-start.1 = (bf16[8,128]{1,0:T(8,128)(2,1)S(1)}, bf16[8,128]{1,0:T(8,128)(2,1)}, u32[]{:S(2)}) copy-start(bf16[8,128]{1,0:T(8,128)(2,1)} %context_ref.1) | copy-start | bytes 6148

commit v5 on v4

--- a/solution.py
+++ b/solution.py
@@ -44,8 +44,7 @@
     turned = pltpu.roll(panel, shift, 1)
     rest = a[PANEL:]
     out = pltpu.roll(jnp.where(rest_lane < PANEL, 0.0, rest), shift, 1)
-    for j in range(PANEL):
-        out = out - rest[:, j : j + 1] * turned[j : j + 1]
+    out = out - dot32(rest[:, :PANEL], turned, ((1,), (0,)))
     return jnp.concatenate([out, turned], axis=0)
 
 

time: 53.7 us -> 59 us (1.099)
  Pallas kernels: 49.3 us -> 55 us
    pallas_call x1, Pallas kernels: 49.3 us -> 55 us  [shards(): pl.pallas_call(functools.partial(sweep, n_pert, n_gene), out_shape=(jax.S...]
where the time goes in v5:
time: 59 us; the launch traced here: 58.6 us
  Pallas kernels  55 us (93%)
  local copies, waits for them, and re-layouts  2.98 us (5%)
  between operations  0.65 us (1%)
    pallas_call x1, Pallas kernels, shards(): pl.pallas_call(functools.partial(sweep, n_pert, n_gene), out_shape=(jax.S...  55 us
    unnamed x6, local copies, waits for them, and re-layouts  2.98 us

profile of v5, /device:TPU:0, one launch (start us, length us, event | category | flops | bytes accessed | tf_op | source)
XLA Modules:
  0.0 58.6 jit_solution(15791398389963467243)
XLA Ops:
  0.6 0.0 copy-start
  0.6 0.9 %copy-done = bf16[1024,128]{1,0:T(8,128)(2,1)S(1)} copy-done((bf16[1024,128]{1,0:T(8,128)(2,1)S(1)}, bf16[1024,128]{1,0:T(8,128)(2,1)}, u32[]{:S(2)}) %copy-start) | copy-done | bytes 262168
  1.6 0.0 copy-start.1
  1.6 0.7 %copy-done.1 = bf16[8,128]{1,0:T(8,128)(2,1)S(1)} copy-done((bf16[8,128]{1,0:T(8,128)(2,1)S(1)}, bf16[8,128]{1,0:T(8,128)(2,1)}, u32[]{:S(2)}) %copy-start.1) | copy-done | bytes 2072
  2.3 55.0 %sweep.1 = (bf16[512,128]{1,0:T(8,128)(2,1)S(1)}, bf16[1024,128]{1,0:T(8,128)(2,1)S(1)}) custom-call(bf16[8192,512]{1,0:T(8,128)(2,1)} %bitcast.1, bf16[1024,128]{1,0:T(8,128)(2,1)S(1)} %copy-done, bf16[8,128]{1,0:T(8,128)(2,1)S(1)} %copy-done.1), custom_call_target="tpu_custom_call" | custom-call | tf_op jit(solution)/shard_map/sweep/pallas_call | solution.py:340
  57.2 0.7 %copy.7 = bf16[512,128]{1,0:T(8,128)(2,1)} copy(bf16[512,128]{1,0:T(8,128)(2,1)S(1)} %get-tuple-element.4) | data formatting | bytes 262144
  57.9 0.7 %copy.8 = bf16[1024,128]{1,0:T(8,128)(2,1)} copy(bf16[1024,128]{1,0:T(8,128)(2,1)S(1)} %get-tuple-element.5) | data formatting | bytes 524288
Async XLA Ops:
  0.6 1.0 %copy-start = (bf16[1024,128]{1,0:T(8,128)(2,1)S(1)}, bf16[1024,128]{1,0:T(8,128)(2,1)}, u32[]{:S(2)}) copy-start(bf16[1024,128]{1,0:T(8,128)(2,1)} %factor_ref.1) | copy-start | bytes 786436
  1.6 0.7 %copy-start.1 = (bf16[8,128]{1,0:T(8,128)(2,1)S(1)}, bf16[8,128]{1,0:T(8,128)(2,1)}, u32[]{:S(2)}) copy-start(bf16[8,128]{1,0:T(8,128)(2,1)} %context_ref.1) | copy-start | bytes 6148
